TPU v7x, 32 devices: a whole 2x2x4 slice. The times are simulated.
32 devices in a mesh: groups: 2 (over x), row: 8 (over z, y), col: 2 (over core).
Axes of the slice: x: 2, y: 2, z: 4, core: 2. Of those that a mesh axis runs over, the one named last changes fastest.
Arguments:
- right_side: float32 [32, 4096], P('groups', ('row', 'col')), parts along dimension 0, may hold values from -6 to 6
- current_ratio: float32 [8192], P(('groups', 'row', 'col')), parts along dimension 0, may hold values from 0.7 to 1
- filament_xy: float32 [2, 6400], replicated, may hold values from -0.3 to 0.3
- element_offset: float32 [2, 8192], P(None, 'groups'), parts along dimension 1, may hold values from -0.003 to 0.003
- element_filament: int32 [8192], P('groups'), parts along dimension 0, may hold values from 0 to 6399
- element_order: int32 [8192], P('groups'), parts along dimension 0, may hold values from 0 to 4095, each once
Outputs:
- solution: float32 [32, 4096], P('groups', ('row', 'col')), parts along dimension 0
- residual: float32 [32, 4096], P('groups', ('row', 'col')), parts along dimension 0
There are 2 independent parts, one for each index of `groups`. A program takes and returns all parts, laid end to end along the dimension named above; an argument that names none is the same for every part. Nothing has to cross between parts.
Inputs may be any that keep to these rules, and one draw needn't show every extreme that they name: `element_order`: each position appears once.
All inputs are finite; a program needn't handle non-finite values.
Results may differ from a plain program's by a relative error of at most 0.00014.
Values sent between devices are 32-bit elements; how exact they have to be, the bound alone decides.
A program may use at most 128 MiB of HBM per device.

v0:
```python
import math
import jax
import jax.numpy as jnp
from jax import lax
from jax.sharding import PartitionSpec as P

ITERS = 2
EPS_SQUARED = 0.0001
COUPLE = 0.3


def kernel(left_x, left_y, right_x, right_y):
    delta_x = left_x[:, None] - right_x[None, :]
    delta_y = left_y[:, None] - right_y[None, :]
    return lax.rsqrt(delta_x * delta_x + delta_y * delta_y + EPS_SQUARED)


def on_device(
    right_side, current_ratio, filament_xy, element_offset, element_filament, element_order
):
    row_devices = lax.axis_size("row")
    col_devices = lax.axis_size("col")
    side_count = right_side.shape[0]
    local_count = right_side.shape[1]
    element_count = local_count * row_devices * col_devices
    coupling_scale = COUPLE / math.sqrt(element_count)
    places = filament_xy[:, element_filament[element_order]] + element_offset[:, element_order]
    diagonal = 1.0 + 8.0 * current_ratio**24
    row_index = lax.axis_index("row")
    col_index = lax.axis_index("col")
    col_width = local_count * col_devices
    col_xy = lax.dynamic_slice_in_dim(places, row_index * col_width, col_width, 1)
    row_xy = lax.dynamic_index_in_dim(
        places.reshape(2, row_devices, col_devices, local_count), col_index, 2, False
    )
    solution = jnp.zeros_like(right_side)
    residual = right_side
    direction = right_side

    def squares(vector):
        return lax.psum(jnp.sum(vector * vector, axis=1, keepdims=True), ("row", "col"))

    norm_now = squares(residual)
    for iteration in range(ITERS):
        wide = lax.all_gather(direction, "col", axis=1, tiled=True)
        peer_count = side_count * lax.axis_size("row") // side_count
        group_size = math.gcd(peer_count, 8)
        blocks = peer_count // group_size
        block_places = row_xy.reshape(2, blocks, group_size * local_count).transpose(1, 0, 2)

        def apply_block(block_xy):
            coupling = kernel(col_xy[0], col_xy[1], block_xy[0], block_xy[1])
            return jnp.dot(
                wide, coupling, precision=lax.Precision.HIGHEST, preferred_element_type=jnp.float32
            )

        parts = lax.map(apply_block, block_places)
        parts = parts.reshape(blocks, side_count, group_size, local_count).transpose(0, 2, 1, 3)
        summed = lax.psum_scatter(
            parts.reshape(peer_count * side_count, local_count),
            "row",
            scatter_dimension=0,
            tiled=True,
        )
        image_vec = diagonal * direction + coupling_scale * summed
        curved = lax.psum(jnp.sum(direction * image_vec, axis=1, keepdims=True), ("row", "col"))
        step_length = norm_now / curved
        solution = solution + step_length * direction
        residual = residual - step_length * image_vec
        norm_next = squares(residual)
        direction = residual + norm_next / norm_now * direction
        norm_now = norm_next
    return (solution, residual)


def solution(mesh):
    return jax.shard_map(
        on_device,
        mesh=mesh,
        in_specs=(
            P("groups", ("row", "col")),
            P(("groups", "row", "col")),
            P(),
            P(None, "groups"),
            P("groups"),
            P("groups"),
        ),
        out_specs=(P("groups", ("row", "col")), P("groups", ("row", "col"))),
        check_vma=False,
    )
```

profile of v0, /device:TPU:0, one launch (start us, length us, event | category | flops | bytes accessed | tf_op | source)
XLA Modules:
  0.0 302.2 jit_solution(8599823185604984722)
XLA Ops:
  7.2 0.7 fusion.12
  8.0 23.0 %gather_fusion = s32[4096]{0:T(1024)S(1)} fusion(s32[4096]{0:T(1024)S(1)} %copy-done, s32[4096]{0:T(1024)S(1)} %fusion.12), kind=kCustom, calls=%fused_computation | custom fusion | bytes 49152 | tf_op jit(solution)/shard_map/gather | solution.py:27
  31.1 1.1 copy.12
  32.2 2.0 copy.13
  34.1 15.7 %gather_fusion.2 = f32[4096,2]{1,0:T(8,128)} fusion(f32[2,4096]{0,1:T(8,128)} %copy.13, s32[4096]{0:T(1024)S(1)} %fusion.12), kind=kCustom, calls=%fused_computation.2 | custom fusion | bytes 81920 | tf_op jit(solution)/shard_map/gather | solution.py:27
  49.8 14.1 %gather_fusion.1 = f32[4096,2]{1,0:T(8,128)} fusion(f32[2,6400]{0,1:T(8,128)S(1)} %copy.12, s32[4096]{0:T(1024)S(1)} %broadcast_clamp_fusion), kind=kCustom, calls=%fused_computation.1 | custom fusion | bytes 81920 | tf_op jit(solution)/shard_map/gather | solution.py:27
  63.9 2.4 add.92
  66.7 0.9 dynamic-slice_reduce_fusion.1
  67.6 1.9 all_gather.6
  69.6 3.2 %fusion.1 = f32[2048,16]{0,1:T(8,128)S(1)} fusion(f32[16,512]{1,0:T(8,128)S(1)} %all_gather.6, f32[2048]{0:T(1024)S(1)} %bitcast.53, f32[512]{0:T(512)S(1)} %get-tuple-element.30, f32[2048]{0:T(1024)S(1)} %bitcast.51, f32[512]{0:T(512)S(1)} %get-tuple-element.24), kind=kOutput, calls=%fused_computation.5 | convolution fusion | flops 207618048 | bytes 184320 | tf_op jit(solution)/shard_map/while/body/eval_jaxpr/dot_general | solution.py:53
  72.9 0.7 copy.15
  73.7 63.9 %reduce-scatter.3.cloned.1.call-done = f32[16,256]{1,0:T(8,128)} async-done(((f32[128,256]{1,0:T(8,128)}), f32[16,256]{1,0:T(8,128)}) %reduce-scatter.3.cloned.1.call-update) | async-done | bytes 16400 | tf_op jit(solution)/shard_map/reduce_scatter | solution.py:59
  137.6 0.8 multiply_reduce_fusion.2
  138.4 29.7 %all-reduce = (f32[16,1]{0,1:T(1,128)S(1)}, f32[16,1]{0,1:T(1,128)S(1)}) all-reduce(f32[16,1]{0,1:T(1,128)S(1)} %bitcast.56, f32[16,1]{0,1:T(1,128)S(1)} %bitcast.55), channel_id=1, replica_groups=mesh['groups'=2,'row'=8,'col'=2] {'row','col'}, use_global_device_ids=true, to_apply=%region_1.2 | all-reduce | flops 32 | bytes 256 | tf_op jit(solution)/shard_map/psum | solution.py:41
  168.1 0.9 multiply_reduce_fusion.1
  169.0 29.5 %psum.30 = f32[16,1]{0,1:T(1,128)S(1)} all-reduce(f32[16,1]{0,1:T(1,128)S(1)} %bitcast.57), channel_id=1, replica_groups=mesh['groups'=2,'row'=8,'col'=2] {'row','col'}, use_global_device_ids=true, to_apply=%region_6.7 | all-reduce | flops 16 | bytes 128 | tf_op jit(solution)/shard_map/psum | solution.py:41
  198.5 0.8 multiply_add_fusion.2
  199.3 1.8 all_gather.7
  201.1 3.1 %fusion = f32[16,2048]{1,0:T(8,128)S(1)} fusion(f32[16,512]{1,0:T(8,128)S(1)} %all_gather.7, f32[2048]{0:T(1024)S(1)} %bitcast.54, f32[512]{0:T(512)S(1)} %get-tuple-element.30, f32[2048]{0:T(1024)S(1)} %bitcast.52, f32[512]{0:T(512)S(1)} %get-tuple-element.24), kind=kOutput, calls=%fused_computation.4 | convolution fusion | flops 207618048 | bytes 184320 | tf_op jit(solution)/shard_map/while/body/eval_jaxpr/dot_general | solution.py:53
  204.2 0.7 copy.16
  204.9 58.5 %reduce-scatter.5.cloned.1.call-done = f32[16,256]{1,0:T(8,128)} async-done(((f32[128,256]{1,0:T(8,128)}), f32[16,256]{1,0:T(8,128)}) %reduce-scatter.5.cloned.1.call-update) | async-done | bytes 16400 | tf_op jit(solution)/shard_map/reduce_scatter | solution.py:59
  263.4 0.8 multiply_reduce_fusion
  264.3 29.6 %psum.31 = f32[16,1]{0,1:T(1,128)S(1)} all-reduce(f32[16,1]{0,1:T(1,128)S(1)} %bitcast.58), channel_id=1, replica_groups=mesh['groups'=2,'row'=8,'col'=2] {'row','col'}, use_global_device_ids=true, to_apply=%region_9.10 | all-reduce | flops 16 | bytes 128 | tf_op jit(solution)/shard_map/psum | solution.py:66
  293.9 1.4 multiply_subtract_fusion
  (30 shorter events, 0.7 us)
Async XLA Ops:
  7.2 0.8 copy-start
  7.2 130.4 %reduce-scatter.3.cloned.1.call-start = ((), (), s32[]{:S(2)}) async-start(), calls=%async_computation.2 | async-start | bytes 147456 | tf_op jit(solution)/shard_map/reduce_scatter | solution.py:59
  8.0 23.1 %copy-start.3 = (f32[2,6400]{1,0:T(2,128)S(1)}, f32[2,6400]{1,0:T(2,128)}, u32[]{:S(2)}) copy-start(f32[2,6400]{1,0:T(2,128)} %param.8) | copy-start | bytes 153604
  31.0 1.2 copy-start.4
  63.9 3.7 %copy-start.1 = (f32[16,256]{1,0:T(8,128)S(1)}, f32[16,256]{1,0:T(8,128)}, u32[]{:S(2)}) copy-start(f32[16,256]{1,0:T(8,128)} %param.6) | copy-start | bytes 49156
  69.6 4.1 %copy-start.5 = (f32[256]{0:T(256)S(1)}, f32[256]{0:T(256)}, u32[]{:S(2)}) copy-start(f32[256]{0:T(256)} %param.7) | copy-start | bytes 3076
  73.6 189.9 %reduce-scatter.5.cloned.1.call-start = ((), (), s32[]{:S(2)}) async-start(), calls=%async_computation.3 | async-start | bytes 147456 | tf_op jit(solution)/shard_map/reduce_scatter | solution.py:59
  201.1 92.9 %copy-start.2 = (f32[16,256]{1,0:T(8,128)S(1)}, f32[16,256]{1,0:T(8,128)}, u32[]{:S(2)}) copy-start(f32[16,256]{1,0:T(8,128)} %reduce-scatter.3.cloned.1.call-done) | copy-start | bytes 49156
Sparse Core Ops, SparseCore 0:
  73.7 63.8 reduce-scatter.2
  205.0 58.3 reduce-scatter.4
where the time goes:
time: 303 us; the launch traced here: 302 us
  waiting for transfers between devices  122 us (40%)
  blocking collectives  92.5 us (31%)
  local copies, waits for them, and re-layouts  58.6 us (19%)
  between operations  14.2 us (5%)
  other arithmetic  8 us (3%)
  matrix products  6.3 us (2%)
    reduce_scatter x2, waiting for transfers between devices, on_device(): lax.psum_scatter(parts.reshape(peer_count * side_count, local_count), 'ro...  122 us
    psum x2, blocking collectives, squares(): lax.psum(jnp.sum(vector * vector, axis=1, keepdims=True), ('row', 'col'))  59.1 us
    psum x1, blocking collectives, on_device(): lax.psum(jnp.sum(direction * image_vec, axis=1, keepdims=True), ('row', '...  29.6 us
    gather x1, local copies, waits for them, and re-layouts, on_device(): element_filament[element_order]  23 us
    gather x1, local copies, waits for them, and re-layouts, on_device(): element_offset[:, element_order]  15.7 us
    gather x1, local copies, waits for them, and re-layouts, on_device(): filament_xy[:, element_filament[element_order]]  14.1 us
    dot_general x2, matrix products, apply_block(): jnp.dot(wide, coupling, precision=lax.Precision.HIGHEST, preferred_elemen...  6.3 us
  transfers between devices with their start and end apart: 2, of which 2 were waited for; matrix products, arithmetic and copies ran while one was open for 0% of the time, Pallas kernels for 0%

commit v1 on v0

--- a/solution.py
+++ b/solution.py
@@ -63,7 +63,9 @@
             tiled=True,
         )
         image_vec = diagonal * direction + coupling_scale * summed
-        curved = lax.psum(jnp.sum(direction * image_vec, axis=1, keepdims=True), ("row", "col"))
+        curved = lax.psum(
+            lax.psum(jnp.sum(direction * image_vec, axis=1, keepdims=True), "col"), "row"
+        )
         step_length = norm_now / curved
         solution = solution + step_length * direction
         residual = residual - step_length * image_vec

time: 303 us -> 317 us (1.046)
  blocking collectives: 92.5 us -> 106 us
    psum x1 -> x4, blocking collectives: 29.6 us -> 41.5 us  [the longest x2 36.5 us: on_device(): lax.psum(lax.psum(jnp.sum(direction * image_vec, axis=1, keepdims=True),...]
where the time goes in v1:
time: 317 us; the launch traced here: 316 us
  waiting for transfers between devices  123 us (39%)
  blocking collectives  106 us (33%)
  local copies, waits for them, and re-layouts  58.6 us (18%)
  between operations  14.2 us (4%)
  other arithmetic  8 us (3%)
  matrix products  6.3 us (2%)
    reduce_scatter x2, waiting for transfers between devices, on_device(): lax.psum_scatter(parts.reshape(peer_count * side_count, local_count), 'ro...  123 us
    psum x2, blocking collectives, squares(): lax.psum(jnp.sum(vector * vector, axis=1, keepdims=True), ('row', 'col'))  61 us
    psum x2, blocking collectives, on_device(): lax.psum(lax.psum(jnp.sum(direction * image_vec, axis=1, keepdims=True),...  36.5 us
    gather x1, local copies, waits for them, and re-layouts, on_device(): element_filament[element_order]  23 us
    gather x1, local copies, waits for them, and re-layouts, on_device(): element_offset[:, element_order]  15.7 us
    gather x1, local copies, waits for them, and re-layouts, on_device(): filament_xy[:, element_filament[element_order]]  14.1 us
  transfers between devices with their start and end apart: 2, of which 2 were waited for; matrix products, arithmetic and copies ran while one was open for 0% of the time, Pallas kernels for 0%

profile of v1, /device:TPU:0, one launch (start us, length us, event | category | flops | bytes accessed | tf_op | source)
XLA Modules:
  0.0 316.1 jit_solution(6051255472083876375)
XLA Ops:
  8.0 23.0 %gather_fusion = s32[4096]{0:T(1024)S(1)} fusion(s32[4096]{0:T(1024)S(1)} %copy-done, s32[4096]{0:T(1024)S(1)} %fusion.12), kind=kCustom, calls=%fused_computation | custom fusion | bytes 49152 | tf_op jit(solution)/shard_map/gather | solution.py:27
  31.1 1.1 copy.12
  32.2 2.0 copy.13
  34.1 15.7 %gather_fusion.2 = f32[4096,2]{1,0:T(8,128)} fusion(f32[2,4096]{0,1:T(8,128)} %copy.13, s32[4096]{0:T(1024)S(1)} %fusion.12), kind=kCustom, calls=%fused_computation.2 | custom fusion | bytes 81920 | tf_op jit(solution)/shard_map/gather | solution.py:27
  49.8 14.1 %gather_fusion.1 = f32[4096,2]{1,0:T(8,128)} fusion(f32[2,6400]{0,1:T(8,128)S(1)} %copy.12, s32[4096]{0:T(1024)S(1)} %broadcast_clamp_fusion), kind=kCustom, calls=%fused_computation.1 | custom fusion | bytes 81920 | tf_op jit(solution)/shard_map/gather | solution.py:27
  63.9 2.4 add.96
  66.7 0.9 dynamic-slice_reduce_fusion.1
  67.6 1.9 all_gather.6
  69.6 3.2 %fusion.1 = f32[2048,16]{0,1:T(8,128)S(1)} fusion(f32[16,512]{1,0:T(8,128)S(1)} %all_gather.6, f32[2048]{0:T(1024)S(1)} %bitcast.53, f32[512]{0:T(512)S(1)} %get-tuple-element.30, f32[2048]{0:T(1024)S(1)} %bitcast.51, f32[512]{0:T(512)S(1)} %get-tuple-element.24), kind=kOutput, calls=%fused_computation.5 | convolution fusion | flops 207618048 | bytes 184320 | tf_op jit(solution)/shard_map/while/body/eval_jaxpr/dot_general | solution.py:53
  73.7 63.9 %reduce-scatter.3.cloned.1.call-done = f32[16,256]{1,0:T(8,128)} async-done(((f32[128,256]{1,0:T(8,128)}), f32[16,256]{1,0:T(8,128)}) %reduce-scatter.3.cloned.1.call-update) | async-done | bytes 16400 | tf_op jit(solution)/shard_map/reduce_scatter | solution.py:59
  137.6 0.8 multiply_reduce_fusion.2
  138.4 2.5 psum.43
  140.9 31.6 %psum.42 = f32[16,1]{0,1:T(1,128)S(1)} all-reduce(f32[16,1]{0,1:T(1,128)S(1)} %bitcast.55), channel_id=1, replica_groups=mesh['groups'=2,'row'=8,'col'=2] {'row','col'}, use_global_device_ids=true, to_apply=%region_1.2 | all-reduce | flops 16 | bytes 128 | tf_op jit(solution)/shard_map/psum | solution.py:41
  172.4 17.1 %psum.44 = f32[16,1]{0,1:T(1,128)S(1)} all-reduce(f32[16,1]{0,1:T(1,128)S(1)} %psum.43), channel_id=1, replica_groups=mesh['groups'=2,'row'=8,'col'=2] {'row'}, use_global_device_ids=true, to_apply=%region_5.6 | all-reduce | flops 16 | bytes 128 | tf_op jit(solution)/shard_map/psum | solution.py:66
  189.6 0.9 multiply_reduce_fusion.1
  190.5 29.5 %psum.45 = f32[16,1]{0,1:T(1,128)S(1)} all-reduce(f32[16,1]{0,1:T(1,128)S(1)} %bitcast.57), channel_id=1, replica_groups=mesh['groups'=2,'row'=8,'col'=2] {'row','col'}, use_global_device_ids=true, to_apply=%region_7.8 | all-reduce | flops 16 | bytes 128 | tf_op jit(solution)/shard_map/psum | solution.py:41
  220.0 0.8 multiply_add_fusion.2
  220.7 1.8 all_gather.7
  222.6 3.1 fusion
  226.4 58.7 %reduce-scatter.5.cloned.1.call-done = f32[16,256]{1,0:T(8,128)} async-done(((f32[128,256]{1,0:T(8,128)}), f32[16,256]{1,0:T(8,128)}) %reduce-scatter.5.cloned.1.call-update) | async-done | bytes 16400 | tf_op jit(solution)/shard_map/reduce_scatter | solution.py:59
  285.1 0.8 multiply_reduce_fusion
  285.9 2.5 psum.46
  288.4 19.4 %psum.47 = f32[16,1]{0,1:T(1,128)S(1)} all-reduce(f32[16,1]{0,1:T(1,128)S(1)} %psum.46), channel_id=1, replica_groups=mesh['groups'=2,'row'=8,'col'=2] {'row'}, use_global_device_ids=true, to_apply=%region_11.12 | all-reduce | flops 16 | bytes 128 | tf_op jit(solution)/shard_map/psum | solution.py:66
  307.8 1.4 multiply_subtract_fusion
  (33 shorter events, 2.7 us)
Async XLA Ops:
  7.2 0.8 copy-start
  7.2 130.4 %reduce-scatter.3.cloned.1.call-start = ((), (), s32[]{:S(2)}) async-start(), calls=%async_computation.2 | async-start | bytes 147456 | tf_op jit(solution)/shard_map/reduce_scatter | solution.py:59
  8.0 23.1 %copy-start.3 = (f32[2,6400]{1,0:T(2,128)S(1)}, f32[2,6400]{1,0:T(2,128)}, u32[]{:S(2)}) copy-start(f32[2,6400]{1,0:T(2,128)} %param.8) | copy-start | bytes 153604
  31.0 1.2 copy-start.4
  63.9 3.7 %copy-start.1 = (f32[16,256]{1,0:T(8,128)S(1)}, f32[16,256]{1,0:T(8,128)}, u32[]{:S(2)}) copy-start(f32[16,256]{1,0:T(8,128)} %param.6) | copy-start | bytes 49156
  69.6 4.1 %copy-start.5 = (f32[256]{0:T(256)S(1)}, f32[256]{0:T(256)}, u32[]{:S(2)}) copy-start(f32[256]{0:T(256)} %param.7) | copy-start | bytes 3076
  73.6 211.5 %reduce-scatter.5.cloned.1.call-start = ((), (), s32[]{:S(2)}) async-start(), calls=%async_computation.3 | async-start | bytes 147456 | tf_op jit(solution)/shard_map/reduce_scatter | solution.py:59
  222.6 85.2 %copy-start.2 = (f32[16,256]{1,0:T(8,128)S(1)}, f32[16,256]{1,0:T(8,128)}, u32[]{:S(2)}) copy-start(f32[16,256]{1,0:T(8,128)} %reduce-scatter.3.cloned.1.call-done) | copy-start | bytes 49156
Sparse Core Ops, SparseCore 0:
  73.7 63.8 reduce-scatter.2
  226.5 58.4 reduce-scatter.4
